TPU v7x, 32 devices: a whole 2x2x4 slice. The times are simulated.
32 devices in a mesh: kz: 8 (over y, x, core), pw: 4 (over z).
Axes of the slice: x: 2, y: 2, z: 4, core: 2. Of those that a mesh axis runs over, the one named last changes fastest.
Arguments:
- states: bfloat16 [8, 2, 384, 512, 128], P('kz', None, None, 'pw'), may hold values from -1.25 to 1.25
- stick_perm: int32 [512], P('pw'), may hold values from 0 to 511, as said below
Outputs:
- margin: float32 [384, 8, 2, 384], P('pw', 'kz')
Inputs may be any that keep to these rules, and one draw needn't show every extreme that they name: `stick_perm`: each aligned run of 128 entries, starting at a multiple of 128, is a permutation of the stick numbers of that run.
All inputs are finite; a program needn't handle non-finite values.
Results may differ from a plain program's by a relative error of at most 0.0003.
Values may be sent and summed in bfloat16 or wider, within the bound.
A program may use at most 192 MiB of HBM per device.

v0:
```python
import jax
import jax.numpy as jnp
from jax import lax
from jax.sharding import PartitionSpec as P


def from_behind(value, axis, steps):
    count = lax.axis_size(axis)
    pairs = [(source, (source + steps) % count) for source in range(count)]
    return lax.ppermute(value, axis, pairs)


def wrap_shift(state, local_perm):
    moved = jnp.take(state, local_perm, axis=2)
    return jnp.concatenate([moved[..., 1:], jnp.zeros_like(moved[..., :1])], axis=-1)


def pair_block(left_rows, right_full):
    products = jnp.einsum(
        "kamp,kbnp->mkabn", left_rows, right_full, preferred_element_type=jnp.float32
    )
    real_part = products[:, :, 0, 0] + products[:, :, 1, 1]
    imag_part = products[:, :, 0, 1] - products[:, :, 1, 0]
    return jnp.stack([real_part, imag_part], axis=2)


def shards(states, stick_perm):
    kpoints = states.shape[0]
    bands = states.shape[2]
    sticks = states.shape[3]
    flat_states = states.reshape(kpoints, 2, bands, -1)
    kz_index = lax.axis_index("kz")
    local_perm = stick_perm - lax.axis_index("pw") * sticks
    wrapped = wrap_shift(states[0], local_perm)
    sent = jnp.where(kz_index == 0, wrapped, states[0])
    arrived = from_behind(sent, "kz", -1)
    arrived_flat = arrived.reshape(1, 2, bands, -1)
    inner = pair_block(flat_states[:-1], flat_states[1:])
    edge = pair_block(flat_states, arrived_flat)
    return lax.psum_scatter(
        jnp.concatenate([inner, edge], axis=1), "pw", scatter_dimension=0, tiled=True
    )


def solution(mesh):
    in_specs = (P("kz", None, None, "pw", None), P("pw"))
    out_specs = P("pw", "kz", None, None)
    return jax.shard_map(shards, mesh=mesh, in_specs=in_specs, out_specs=out_specs, check_vma=False)
```

profile of v0, /device:TPU:1, one launch (start us, length us, event | category | flops | bytes accessed | tf_op | source)
XLA Modules:
  0.0 541.2 jit_solution(18238220644067041877)
XLA Ops:
  6.5 0.0 all-reduce.4.cloned.1.call-start
  6.5 0.7 compare_and_fusion
  7.2 26.9 %copy.13 = bf16[2,384,128,128]{3,1,2,0:T(8,128)(2,1)} copy(bf16[2,384,128,128]{3,2,1,0:T(8,128)(2,1)} %bitcast.34) | data formatting | bytes 50331648 | tf_op jit(solution)/shard_map/squeeze | solution.py:34
  34.1 19.2 %gather_fusion = bf16[128,2,384,128]{3,2,1,0:T(8,128)(2,1)} fusion(bf16[2,384,128,128]{3,1,2,0:T(8,128)(2,1)} %copy.13, s32[1024]{0:T(1024)S(1)} %pad_clamp_fusion), kind=kCustom, calls=%fused_computation | custom fusion | bytes 50332160 | tf_op jit(solution)/shard_map/jit(_take)/gather | solution.py:14
  53.3 12.7 %select_bitcast_fusion = bf16[2,384,128,128]{3,1,0,2:T(8,128)(2,1)S(1)} fusion(bf16[128,2,384,128]{3,2,1,0:T(8,128)(2,1)} %gather_fusion, pred[128]{0:T(512)(128)(4,1)S(1)} %get-tuple-element.5), kind=kLoop, calls=%fused_computation.4 | loop fusion | flops 12582912 | bytes 50331776 | tf_op jit(solution)/shard_map/jit(_take)/select_n | solution.py:14
  66.0 12.7 %slice.22 = bf16[2,384,128,127]{3,1,0,2:T(8,128)(2,1)} slice(bf16[2,384,128,128]{3,1,0,2:T(8,128)(2,1)S(1)} %select_bitcast_fusion), slice={[0:2], [0:384], [0:128], [1:128]} | slice | bytes 49938432 | tf_op jit(solution)/shard_map/slice | solution.py:15
  78.7 30.8 %bitcast_select_fusion = bf16[2,384,128,128]{3,1,0,2:T(8,128)(2,1)} fusion(bf16[1,2,384,128,128]{4,3,2,1,0:T(8,128)(2,1)} %param.2, bf16[2,384,128,127]{3,1,0,2:T(8,128)(2,1)} %slice.22, pred[]{:T(512)S(6)} %eq.3), kind=kLoop, calls=%fused_computation.3 | loop fusion | flops 12582912 | bytes 75300864 | tf_op jit(solution)/shard_map/jit(_where)/select_n | solution.py:35
  109.6 0.1 collective-permute-start
  109.6 37.3 %reshape.74 = bf16[2,384,16384,1]{2,1,0,3:T(8,128)(2,1)} reshape(bf16[1,2,384,128,128]{4,3,2,1,0:T(8,128)(2,1)} %param.2) | data formatting | bytes 50331648 | tf_op jit(solution)/shard_map/reshape.4
  147.0 236.4 %collective-permute-done = bf16[2,384,128,128]{3,1,0,2:T(8,128)(2,1)} collective-permute-done((bf16[2,384,128,128]{3,1,0,2:T(8,128)(2,1)}, bf16[2,384,128,128]{3,1,0,2:T(8,128)(2,1)}, u32[]{:S(2)}, u32[]{:S(2)}) %collective-permute-start) | collective-permute-done | bytes 25165856 | tf_op jit(solution)/shard_map/ppermute | solution.py:10
  383.4 26.9 %copy.14 = bf16[2,384,128,128]{3,2,1,0:T(8,128)(2,1)} copy(bf16[2,384,128,128]{3,1,0,2:T(8,128)(2,1)} %collective-permute-done) | data formatting | bytes 50331648 | tf_op jit(solution)/shard_map/ppermute | solution.py:10
  410.2 37.4 %reshape.73 = bf16[2,384,16384,1]{2,1,0,3:T(8,128)(2,1)} reshape(bf16[2,384,128,128]{3,2,1,0:T(8,128)(2,1)} %copy.14) | data formatting | bytes 50331648 | tf_op jit(solution)/shard_map/reshape.1
  447.6 0.0 copy-start
  447.6 24.9 %fusion.2 = f32[384,1,2,2,384]{0,4,2,3,1:T(8,128)S(1)} fusion(bf16[2,384,16384,1]{2,1,0,3:T(8,128)(2,1)} %reshape.74, bf16[2,384,16384,1]{2,1,0,3:T(8,128)(2,1)} %reshape.73), kind=kOutput, calls=%fused_computation.5 | convolution fusion | flops 19327352832 | bytes 52690944 | tf_op jit(solution)/shard_map/kamp,kbnp->mkabn/dot_general | solution.py:19
  472.5 0.1 fusion.5
  472.6 0.1 fusion.7
  472.7 0.1 pad_maximum_fusion
  472.8 2.0 copy.17
  474.7 0.0 all-reduce.4.cloned.1.call-update
  474.8 0.0 copy-done
  474.8 0.6 dynamic-slice
  476.0 56.6 %all-reduce.4.cloned.1.call-done = f32[384,1,2,384]{3,2,1,0:T(2,128)} async-done(((f32[384,1,2,384]{3,2,1,0:T(2,128)}), f32[384,1,2,384]{3,2,1,0:T(2,128)}) %all-reduce.4.cloned.1.call-update) | async-done | bytes 1179664
  532.6 1.7 constant_dynamic-slice_fusion
  (1 shorter events, 0.0 us)
Async XLA Ops:
  6.5 526.1 %all-reduce.4.cloned.1.call-start = ((), (), s32[]{:S(2)}) async-start(), calls=%async_computation | async-start | bytes 2359296
  109.6 273.8 %collective-permute-start = (bf16[2,384,128,128]{3,1,0,2:T(8,128)(2,1)}, bf16[2,384,128,128]{3,1,0,2:T(8,128)(2,1)}, u32[]{:S(2)}, u32[]{:S(2)}) collective-permute-start(bf16[2,384,128,128]{3,1,0,2:T(8,128)(2,1)} %bitcast_select_fusion), channel_id=1, source_target_pairs={{0,28},{4,0},{8,4},{12,8},{16,12},{20,16},{24,20},{28,24},{1,29},{... | collective-permute-start | bytes 75497480 | tf_op jit(solution)/shard_map/ppermute | solution.py:10
  447.6 27.2 %copy-start = (u32[32]{0:T(128)S(1)}, u32[32]{0:T(128)}, u32[]{:S(2)}) copy-start(u32[32]{0:T(128)} %constant.34) | copy-start | bytes 388
Sparse Core Ops, SparseCore 0:
  474.9 57.6 all-reduce.3
where the time goes:
time: 544 us; the launch traced here: 541 us
  waiting for transfers between devices  293 us (54%)
  local copies, waits for them, and re-layouts  165 us (30%)
  other arithmetic  44.4 us (8%)
  matrix products  24.9 us (5%)
  between operations  14.1 us (3%)
    ppermute x1, waiting for transfers between devices, from_behind(): return lax.ppermute(value, axis, pairs)  236 us
    another operation x2, local copies, waits for them, and re-layouts  74.7 us
    unnamed x2, waiting for transfers between devices  56.6 us
    select_n x1, other arithmetic, shards(): sent = jnp.where(kz_index == 0, wrapped, states[0])  30.8 us
    squeeze x1, local copies, waits for them, and re-layouts, shards(): wrapped = wrap_shift(states[0], local_perm)  26.9 us
    ppermute x1, local copies, waits for them, and re-layouts, from_behind(): return lax.ppermute(value, axis, pairs)  26.9 us
    dot_general x1, matrix products, pair_block(): jnp.einsum('kamp,kbnp->mkabn', left_rows, right_full, preferred_element_t...  24.9 us
    gather x1, local copies, waits for them, and re-layouts, wrap_shift(): moved = jnp.take(state, local_perm, axis=2)  19.2 us
  transfers between devices with their start and end apart: 2, of which 2 were waited for; matrix products, arithmetic and copies ran while one was open for 7% of the time, Pallas kernels for 0%

commit v1 on v0

v1 whole, which is shorter than its diff:
```python
import functools

import jax
import jax.numpy as jnp
from jax import lax
from jax.experimental import pallas as pl
from jax.experimental.pallas import tpu as pltpu
from jax.sharding import PartitionSpec as P

MESH = pl.DeviceIdType.MESH
GROUP = 16
CHUNK = 64
PIECE = 32
AHEAD = 12


def exchange_matrix():
    row = lax.broadcasted_iota(jnp.int32, (GROUP * GROUP, GROUP * GROUP), 0)
    col = lax.broadcasted_iota(jnp.int32, (GROUP * GROUP, GROUP * GROUP), 1)
    source = (row % GROUP) * GROUP + row // GROUP
    return jnp.where(col == source, 1.0, 0.0).astype(jnp.bfloat16)


def kernel(
    nk, npw, perm_ref, states_ref, out_ref,
    a_flat, a_stage, land, b_flat, acc, part, got, swap,
    load_sem, send_sem, recv_sem, part_send, part_recv,
):
    bands, sticks, length = states_ref.shape[2:]
    chunks = bands // CHUNK
    cuts = sticks // PIECE
    pieces = chunks * cuts
    depth = PIECE * length
    rows = bands // npw
    groups = 2 * bands // GROUP
    kz = lax.axis_index("kz")
    pw = lax.axis_index("pw")
    before = lax.rem(kz + nk - 1, nk)
    after = lax.rem(kz + 1, nk)

    def load(group):
        band = lax.rem(group, groups // 2) * GROUP
        return pltpu.make_async_copy(
            states_ref.at[0, group // (groups // 2), pl.ds(band, GROUP)],
            a_stage.at[lax.rem(group, 2)],
            load_sem.at[lax.rem(group, 2)],
        )

    def send(piece):
        band = (piece // cuts) * CHUNK
        stick = lax.rem(piece, cuts) * PIECE
        return pltpu.make_async_remote_copy(
            src_ref=states_ref.at[0, :, pl.ds(band, CHUNK), pl.ds(stick, PIECE)],
            dst_ref=land.at[piece],
            send_sem=send_sem.at[piece],
            recv_sem=recv_sem.at[piece],
            device_id=(before, pw),
            device_id_type=MESH,
        )

    def share(chunk, step):
        other = lax.rem(pw + step, npw)
        return pltpu.make_async_remote_copy(
            src_ref=part.at[chunk, pl.ds(pl.multiple_of(other * rows, 8), rows)],
            dst_ref=got.at[chunk, step - 1],
            send_sem=part_send.at[chunk, step - 1],
            recv_sem=part_recv.at[chunk, step - 1],
            device_id=(kz, other),
            device_id_type=MESH,
        )

    load(0).start()
    barrier = pltpu.get_barrier_semaphore()
    for neighbour in (before, after):
        pl.semaphore_signal(barrier, inc=1, device_id=(neighbour, pw), device_id_type=MESH)
    for step in range(1, npw):
        other = lax.rem(pw + step, npw)
        pl.semaphore_signal(barrier, inc=1, device_id=(kz, other), device_id_type=MESH)
    pl.semaphore_wait(barrier, npw + 1)

    @pl.loop(0, min(AHEAD, pieces))
    def _(piece):
        send(piece).start()

    swap[...] = exchange_matrix()

    def flatten(block):
        wide = [block[:, s : s + GROUP].reshape(GROUP * GROUP, length) for s in (0, GROUP)]
        moved = jnp.dot(swap[...], jnp.concatenate(wide, axis=1), preferred_element_type=jnp.float32)
        moved = moved.astype(jnp.bfloat16)
        cells = [
            moved[GROUP * s : GROUP * (s + 1), half * length : (half + 1) * length]
            for half in range(2)
            for s in range(GROUP)
        ]
        return jnp.concatenate(cells, axis=1)

    @pl.loop(0, groups)
    def _(group):
        @pl.when(group + 1 < groups)
        def _():
            load(group + 1).start()

        load(group).wait()
        slot = lax.rem(group, 2)

        @pl.when(kz == nk - 1)
        def _():
            local = perm_ref[...] - pw * sticks
            target = lax.broadcasted_iota(jnp.int32, (sticks, sticks), 0)
            place = jnp.where(target == local, 1.0, 0.0).astype(jnp.bfloat16)
            lane = lax.broadcasted_iota(jnp.int32, (sticks, length), 1)
            for band in range(GROUP):
                moved = jnp.dot(place, a_stage[slot, band], preferred_element_type=jnp.float32)
                moved = jnp.where(lane == 0, 0.0, pltpu.roll(moved, 1, 1))
                a_stage[slot, band] = moved.astype(jnp.bfloat16)

        row = pl.multiple_of(group * GROUP, GROUP)
        for cut in range(sticks // (2 * GROUP)):
            block = a_stage[slot, :, cut * 2 * GROUP : (cut + 1) * 2 * GROUP]
            a_flat[pl.ds(row, GROUP), cut * 2 * GROUP * length : (cut + 1) * 2 * GROUP * length] = flatten(block)

    @pl.loop(0, pieces)
    def _(piece):
        chunk = piece // cuts
        cut = lax.rem(piece, cuts)
        send(piece).wait_recv()
        for comp in range(2):
            for group in range(CHUNK // GROUP):
                for part_of in range(PIECE // (2 * GROUP)):
                    block = land[piece, comp, group * GROUP : (group + 1) * GROUP, part_of * 2 * GROUP : (part_of + 1) * 2 * GROUP]
                    row = comp * CHUNK + group * GROUP
                    b_flat[row : row + GROUP, part_of * 2 * GROUP * length : (part_of + 1) * 2 * GROUP * length] = flatten(block)
        at = pl.multiple_of(cut * depth, depth)
        product = lax.dot_general(
            a_flat[:, pl.ds(at, depth)], b_flat[...], (((1,), (1,)), ((), ())),
            preferred_element_type=jnp.float32,
        )

        @pl.when(cut == 0)
        def _():
            acc[...] = product

        @pl.when(cut > 0)
        def _():
            acc[...] += product

        @pl.when(cut == cuts - 1)
        def _():
            total = acc[...]
            turned = pltpu.roll(total[bands:], CHUNK, 1)
            lane = lax.broadcasted_iota(jnp.int32, (bands, 2 * CHUNK), 1)
            part[chunk] = total[:bands] + jnp.where(lane < CHUNK, turned, -turned)
            for step in range(1, npw):
                share(chunk, step).start()

        send(piece).wait_send()

        @pl.when(piece + AHEAD < pieces)
        def _():
            send(piece + AHEAD).start()

    @pl.loop(0, chunks)
    def _(chunk):
        for step in range(1, npw):
            share(chunk, step).wait()
        total = part[chunk, pl.ds(pl.multiple_of(pw * rows, 8), rows)]
        for step in range(1, npw):
            total += got[chunk, step - 1]
        out_ref[chunk] = total


def margins(nk, npw, states, stick_perm):
    _, _, bands, sticks, length = states.shape
    chunks = bands // CHUNK
    pieces = chunks * (sticks // PIECE)
    rows = bands // npw
    blocks = pl.pallas_call(
        functools.partial(kernel, nk, npw),
        out_shape=jax.ShapeDtypeStruct((chunks, rows, 2 * CHUNK), jnp.float32),
        in_specs=[pl.BlockSpec(memory_space=pltpu.VMEM), pl.BlockSpec(memory_space=pl.ANY)],
        out_specs=pl.BlockSpec(memory_space=pltpu.VMEM),
        scratch_shapes=[
            pltpu.VMEM((2 * bands, sticks * length), jnp.bfloat16),
            pltpu.VMEM((2, GROUP, sticks, length), jnp.bfloat16),
            pltpu.VMEM((pieces, 2, CHUNK, PIECE, length), jnp.bfloat16),
            pltpu.VMEM((2 * CHUNK, PIECE * length), jnp.bfloat16),
            pltpu.VMEM((2 * bands, 2 * CHUNK), jnp.float32),
            pltpu.VMEM((chunks, bands, 2 * CHUNK), jnp.float32),
            pltpu.VMEM((chunks, npw - 1, rows, 2 * CHUNK), jnp.float32),
            pltpu.VMEM((GROUP * GROUP, GROUP * GROUP), jnp.bfloat16),
            pltpu.SemaphoreType.DMA((2,)),
            pltpu.SemaphoreType.DMA((pieces,)),
            pltpu.SemaphoreType.DMA((pieces,)),
            pltpu.SemaphoreType.DMA((chunks, npw - 1)),
            pltpu.SemaphoreType.DMA((chunks, npw - 1)),
        ],
        compiler_params=pltpu.CompilerParams(
            collective_id=0, has_side_effects=True, vmem_limit_bytes=60 * 2**20
        ),
        cost_estimate=pl.CostEstimate(
            flops=8 * bands * bands * sticks * length,
            bytes_accessed=4 * states.size,
            transcendentals=0,
        ),
    )(stick_perm.reshape(1, sticks), states)
    split = blocks.reshape(chunks, rows, 2, CHUNK)
    return jnp.transpose(split, (1, 2, 0, 3)).reshape(rows, 1, 2, bands)


def solution(mesh):
    in_specs = (P("kz", None, None, "pw", None), P("pw"))
    out_specs = P("pw", "kz", None, None)
    shards = functools.partial(margins, mesh.shape["kz"], mesh.shape["pw"])
    return jax.shard_map(shards, mesh=mesh, in_specs=in_specs, out_specs=out_specs, check_vma=False)
```

time: 544 us -> 287 us (0.53)
  waiting for transfers between devices: 293 us -> 0 us
  Pallas kernels: 0 us -> 284 us
  local copies, waits for them, and re-layouts: 165 us -> 2.03 us
  other arithmetic: 44.4 us -> 0 us
  matrix products: 24.9 us -> 0 us
  between operations: 14.1 us -> 0.02 us
    pallas_call x0 -> x1, Pallas kernels: none -> 284 us  [margins(): pl.pallas_call(functools.partial(kernel, nk, npw), out_shape=jax.ShapeDty...]
    ppermute x1 -> x0, waiting for transfers between devices: 236 us -> none  [from_behind(): return lax.ppermute(value, axis, pairs)]
    another operation x3 -> x0, local copies, waits for them, and re-layouts: 76.7 us -> none
    unnamed x2 -> x0, waiting for transfers between devices: 56.6 us -> none
    select_n x2 -> x0, other arithmetic: 43.5 us -> none  [the longest x1 30.8 us: shards(): sent = jnp.where(kz_index == 0, wrapped, states[0])]
    squeeze x1 -> x0, local copies, waits for them, and re-layouts: 26.9 us -> none  [shards(): wrapped = wrap_shift(states[0], local_perm)]
    ppermute x1 -> x0, local copies, waits for them, and re-layouts: 26.9 us -> none  [from_behind(): return lax.ppermute(value, axis, pairs)]
    dot_general x1 -> x0, matrix products: 24.9 us -> none  [pair_block(): jnp.einsum('kamp,kbnp->mkabn', left_rows, right_full, preferred_element_t...]
  transfers between devices with their start and end apart: 2 -> 0, of which waited for: 2 -> 0; matrix products, arithmetic and copies ran while one was open for 7% -> 0% of each run, Pallas kernels for 0% -> 0%
where the time goes in v1:
time: 287 us; the launch traced here: 286 us
  Pallas kernels  284 us (99%)
    pallas_call x1, Pallas kernels, margins(): pl.pallas_call(functools.partial(kernel, nk, npw), out_shape=jax.ShapeDty...  284 us

profile of v1, /device:TPU:1, one launch (start us, length us, event | category | flops | bytes accessed | tf_op | source)
XLA Modules:
  0.0 286.5 jit_solution(6088318109638705834)
XLA Ops:
  0.0 284.4 %shard_map.28 = f32[6,96,128]{2,1,0:T(8,128)} custom-call(s32[1,128]{1,0:T(1,128)} %bitcast.7, bf16[1,2,384,128,128]{4,3,2,1,0:T(8,128)(2,1)} %states_ref.1), custom_call_target="tpu_custom_call" | custom-call | flops 19327352832 | bytes 50331648 | tf_op jit(solution)/shard_map/pallas_call | solution.py:178
  284.5 1.1 copy.4
  285.6 0.9 copy.6
  (1 shorter events, 0.0 us)

commit v2 on v1

--- a/solution.py
+++ b/solution.py
@@ -10,8 +10,8 @@
 MESH = pl.DeviceIdType.MESH
 GROUP = 16
 CHUNK = 64
-PIECE = 32
-AHEAD = 12
+PIECE = 16
+AHEAD = 16
 
 
 def exchange_matrix():
@@ -84,16 +84,25 @@
 
     swap[...] = exchange_matrix()
 
-    def flatten(block):
-        wide = [block[:, s : s + GROUP].reshape(GROUP * GROUP, length) for s in (0, GROUP)]
+    def flatten(pair):
+        wide = [block.reshape(GROUP * GROUP, length) for block in pair]
         moved = jnp.dot(swap[...], jnp.concatenate(wide, axis=1), preferred_element_type=jnp.float32)
         moved = moved.astype(jnp.bfloat16)
-        cells = [
-            moved[GROUP * s : GROUP * (s + 1), half * length : (half + 1) * length]
+        return [
+            jnp.concatenate(
+                [moved[GROUP * s : GROUP * (s + 1), half * length : (half + 1) * length] for s in range(GROUP)],
+                axis=1,
+            )
             for half in range(2)
-            for s in range(GROUP)
         ]
-        return jnp.concatenate(cells, axis=1)
+
+    def collect(chunk):
+        for step in range(1, npw):
+            share(chunk, step).wait()
+        total = part[chunk, pl.ds(pl.multiple_of(pw * rows, 8), rows)]
+        for step in range(1, npw):
+            total += got[chunk, step - 1]
+        out_ref[chunk] = total
 
     @pl.loop(0, groups)
     def _(group):
@@ -116,21 +125,27 @@
                 a_stage[slot, band] = moved.astype(jnp.bfloat16)
 
         row = pl.multiple_of(group * GROUP, GROUP)
-        for cut in range(sticks // (2 * GROUP)):
-            block = a_stage[slot, :, cut * 2 * GROUP : (cut + 1) * 2 * GROUP]
-            a_flat[pl.ds(row, GROUP), cut * 2 * GROUP * length : (cut + 1) * 2 * GROUP * length] = flatten(block)
+        for cut in range(0, sticks // GROUP, 2):
+            pair = [a_stage[slot, :, at * GROUP : (at + 1) * GROUP] for at in (cut, cut + 1)]
+            for at, flat in zip((cut, cut + 1), flatten(pair)):
+                a_flat[pl.ds(row, GROUP), at * GROUP * length : (at + 1) * GROUP * length] = flat
 
     @pl.loop(0, pieces)
     def _(piece):
         chunk = piece // cuts
         cut = lax.rem(piece, cuts)
+
+        @pl.when(piece == pieces - 1)
+        def _():
+            pl.loop(0, chunks - 1)(collect)
+
         send(piece).wait_recv()
         for comp in range(2):
-            for group in range(CHUNK // GROUP):
-                for part_of in range(PIECE // (2 * GROUP)):
-                    block = land[piece, comp, group * GROUP : (group + 1) * GROUP, part_of * 2 * GROUP : (part_of + 1) * 2 * GROUP]
-                    row = comp * CHUNK + group * GROUP
-                    b_flat[row : row + GROUP, part_of * 2 * GROUP * length : (part_of + 1) * 2 * GROUP * length] = flatten(block)
+            for group in range(0, CHUNK // GROUP, 2):
+                pair = [land[piece, comp, at * GROUP : (at + 1) * GROUP] for at in (group, group + 1)]
+                for at, flat in zip((group, group + 1), flatten(pair)):
+                    row = comp * CHUNK + at * GROUP
+                    b_flat[row : row + GROUP] = flat
         at = pl.multiple_of(cut * depth, depth)
         product = lax.dot_general(
             a_flat[:, pl.ds(at, depth)], b_flat[...], (((1,), (1,)), ((), ())),
@@ -160,14 +175,7 @@
         def _():
             send(piece + AHEAD).start()
 
-    @pl.loop(0, chunks)
-    def _(chunk):
-        for step in range(1, npw):
-            share(chunk, step).wait()
-        total = part[chunk, pl.ds(pl.multiple_of(pw * rows, 8), rows)]
-        for step in range(1, npw):
-            total += got[chunk, step - 1]
-        out_ref[chunk] = total
+    collect(chunks - 1)
 
 
 def margins(nk, npw, states, stick_perm):

time: 287 us -> 287 us (level)
  no operation moved by 1% of the time
where the time goes in v2:
time: 287 us; the launch traced here: 286 us
  Pallas kernels  284 us (99%)
    pallas_call x1, Pallas kernels, margins(): pl.pallas_call(functools.partial(kernel, nk, npw), out_shape=jax.ShapeDty...  284 us

profile of v2, /device:TPU:1, one launch (start us, length us, event | category | flops | bytes accessed | tf_op | source)
XLA Modules:
  0.0 286.1 jit_solution(4668234873302209872)
XLA Ops:
  0.0 284.1 %shard_map.28 = f32[6,96,128]{2,1,0:T(8,128)} custom-call(s32[1,128]{1,0:T(1,128)} %bitcast.7, bf16[1,2,384,128,128]{4,3,2,1,0:T(8,128)(2,1)} %states_ref.1), custom_call_target="tpu_custom_call" | custom-call | flops 19327352832 | bytes 50331648 | tf_op jit(solution)/shard_map/pallas_call | solution.py:186
  284.1 1.1 copy.4
  285.3 0.9 copy.6
  (1 shorter events, 0.0 us)
